TPU v7x, 32 devices: a whole 2x2x4 slice. The times are simulated.
32 devices in a mesh: groups: 2 (over x), particle: 16 (over z, y, core).
Axes of the slice: x: 2, y: 2, z: 4, core: 2. Of those that a mesh axis runs over, the one named last changes fastest.
Arguments:
- pool: bfloat16 [4096, 2, 8, 1024], P(('groups', 'particle')), parts along dimension 0, may hold values from -6 to 6
- page_table: int32 [2048, 2], P(('groups', 'particle')), parts along dimension 0, may hold values from 0 to 127, as said below
- lengths: int32 [2048], P('groups'), parts along dimension 0, may hold values from 1 to 15
- ancestors: int32 [2048], P('groups'), parts along dimension 0, may hold values from 0 to 1023, as said below
- new_q: bfloat16 [2048, 8192], P(('groups', 'particle')), parts along dimension 0, may hold values from -70 to 70
- new_kv: bfloat16 [2048, 2, 1024], P(('groups', 'particle')), parts along dimension 0, may hold values from -6 to 6
- score_weight: float32 [8192], replicated, may hold values from -3 to 3
Outputs:
- new_pool: bfloat16 [4096, 2, 8, 1024], P(('groups', 'particle')), parts along dimension 0
- attn_out: bfloat16 [2048, 8192], P(('groups', 'particle')), parts along dimension 0
- log_weights: float32 [2048], P(('groups', 'particle')), parts along dimension 0
There are 2 independent parts, one for each index of `groups`. A program takes and returns all parts, laid end to end along the dimension named above; an argument that names none is the same for every part. Nothing has to cross between parts.
Inputs may be any that keep to these rules, and one draw needn't show every extreme that they name: page_table's rows of one device together name every slot 0 to 127 once. ancestors[n] belongs to the same prompt as n; among the 64 particles of one device at most 8 have their ancestors on any one device, and some device pair reaches 8.
All inputs are finite; a program needn't handle non-finite values.
Results may differ from a plain program's by a relative error of at most 0.0085.
Values may be sent and summed in bfloat16 or wider, within the bound.
A program may use at most 128 MiB of HBM per device.

v0:
```python
import jax
import jax.numpy as jnp
from jax import lax
from jax.sharding import PartitionSpec as P

HEADS = 64
KV_HEADS = 8
HEAD_DIM = 128
GROUP = 64


def attend(query, held, length_now):
    rows = query.shape[0]
    positions = held.shape[1] * held.shape[3]
    key_rows = held[:, :, 0].reshape(rows, positions, KV_HEADS, HEAD_DIM)
    value_rows = held[:, :, 1].reshape(rows, positions, KV_HEADS, HEAD_DIM)
    grouped = query.reshape(rows, KV_HEADS, HEADS // KV_HEADS, HEAD_DIM)
    scores = jnp.einsum(
        "pgrd,ptgd->pgrt", grouped, key_rows, preferred_element_type=jnp.float32
    ) * HEAD_DIM ** (-0.5)
    visible = jnp.arange(positions, dtype=jnp.int32)[None, :] <= length_now[:, None]
    scores = jnp.where(visible[:, None, None, :], scores, -1e30)
    highest = jnp.max(scores, axis=3, keepdims=True)
    expo = jnp.exp(scores - highest)
    probs = (expo / jnp.sum(expo, axis=3, keepdims=True)).astype(jnp.bfloat16)
    mixed_heads = jnp.einsum(
        "pgrt,ptgd->pgrd", probs, value_rows, preferred_element_type=jnp.float32
    )
    return mixed_heads.reshape(rows, HEADS * HEAD_DIM).astype(jnp.bfloat16)


def local(pool, page_table, lengths, ancestors, new_q, new_kv, score_weight):
    devices = lax.axis_size("particle")
    self_index = lax.axis_index("particle")
    per_device = new_q.shape[0]
    page_count = page_table.shape[1]
    page_len = pool.shape[2]
    kv_width = pool.shape[3]
    prompts = devices * per_device // GROUP
    stride = max(1, prompts // per_device)
    reach_size = devices // stride
    capacity = 2 * per_device // reach_size
    held_pages = pool[page_table]
    anc_all = ancestors.reshape(devices, per_device)
    anc_dev = anc_all // per_device
    row_order = jnp.arange(per_device, dtype=jnp.int32)
    my_sources = lax.dynamic_slice_in_dim(anc_dev, self_index, 1, 0)[0]
    my_ancestors = lax.dynamic_slice_in_dim(anc_all, self_index, 1, 0)[0]
    from_self = anc_dev == self_index
    slot_rank = jnp.cumsum(from_self.astype(jnp.int32), axis=1) - 1
    picked = from_self[:, None, :] & (
        slot_rank[:, None, :] == jnp.arange(capacity, dtype=jnp.int32)[None, :, None]
    )
    source_row = jnp.sum(jnp.where(picked, anc_all[:, None, :] % per_device, 0), axis=2)
    filled = jnp.any(picked, axis=2)
    outgoing = jnp.where(
        filled[:, :, None, None, None, None],
        held_pages[source_row],
        jnp.zeros((), held_pages.dtype),
    )
    incoming = lax.all_to_all(outgoing, "particle", split_axis=0, concat_axis=0, tiled=True)
    earlier = (my_sources[None, :] == my_sources[:, None]) & (
        row_order[None, :] < row_order[:, None]
    )
    arrive_slot = my_sources * capacity + jnp.sum(earlier.astype(jnp.int32), axis=1)
    inherited = incoming.reshape((devices * capacity,) + incoming.shape[2:])[arrive_slot]
    length_now = lengths[my_ancestors]
    position = jnp.arange(page_count * page_len, dtype=jnp.int32).reshape(page_count, page_len)
    at_new = position[None] == length_now[:, None, None]
    descended = jnp.where(at_new[:, :, None, :, None], new_kv[:, None, :, None, :], inherited)
    new_pool = (
        jnp.zeros_like(pool)
        .at[page_table.reshape(-1)]
        .set(descended.reshape(per_device * page_count, 2, page_len, kv_width))
    )
    attn_out = attend(new_q, descended, length_now)
    reward = jnp.sum(attn_out.astype(jnp.float32) * score_weight[None, :], axis=1)
    prompt_ids = (self_index * per_device + row_order) % prompts
    member = prompt_ids[:, None] == jnp.arange(prompts, dtype=jnp.int32)[None, :]
    local_high = jnp.max(jnp.where(member, reward[:, None], -1e30), axis=0)
    highest = lax.pmax(local_high, "particle")
    local_sum = jnp.sum(
        jnp.exp(jnp.where(member, reward[:, None] - highest[None, :], -1e30)), axis=0
    )
    summed = lax.psum(local_sum, "particle")
    normalizer = highest + jnp.log(summed)
    log_weights = reward - jnp.sum(jnp.where(member, normalizer[None, :], 0.0), axis=1)
    return (new_pool, attn_out, log_weights)


def solution(mesh):
    in_specs = (
        P(("groups", "particle"), None, None, None),
        P(("groups", "particle"), None),
        P("groups"),
        P("groups"),
        P(("groups", "particle"), None),
        P(("groups", "particle"), None, None),
        P(),
    )
    out_specs = (
        P(("groups", "particle"), None, None, None),
        P(("groups", "particle"), None),
        P(("groups", "particle")),
    )
    return jax.shard_map(local, mesh=mesh, in_specs=in_specs, out_specs=out_specs, check_vma=False)
```

profile of v0, /device:TPU:0, one launch (start us, length us, event | category | flops | bytes accessed | tf_op | source)
XLA Modules:
  0.0 405.6 jit_solution(4691582920254733234)
XLA Ops:
  0.7 0.8 reshape.276
  1.4 0.2 reduce_window_sum.11
  1.7 0.4 fusion.17
  2.0 0.4 select_reduce_fusion
  2.6 0.7 compare_select_fusion.1
  3.6 5.0 %gather_fusion.1 = bf16[128,2,8,1024]{3,2,1,0:T(8,128)(2,1)} fusion(bf16[128,2,8,1024]{3,2,1,0:T(8,128)(2,1)} %param.7, s32[1024]{0:T(1024)S(1)} %pad_clamp_fusion.2), kind=kCustom, calls=%fused_computation.1 | custom fusion | bytes 8389120 | tf_op jit(solution)/shard_map/gather | solution.py:43
  8.6 8.7 %gather_fusion.2 = bf16[128,2,2,8,1024]{4,3,2,1,0:T(8,128)(2,1)} fusion(bf16[64,2,2,8,1024]{4,3,2,1,0:T(8,128)(2,1)} %bitcast.58, s32[1024]{0:T(1024)S(1)} %pad_clamp_fusion.1), kind=kCustom, calls=%fused_computation.2 | custom fusion | bytes 16777728 | tf_op jit(solution)/shard_map/gather | solution.py:58
  17.3 7.2 %broadcast_select_fusion = bf16[16,8,2,2,8,1024]{5,4,3,2,1,0:T(8,128)(2,1)} fusion(bf16[16,8,2,2,8,1024]{5,4,3,2,1,0:T(8,128)(2,1)} %bitcast.59, pred[16,8]{1,0:T(8,128)(4,1)S(1)} %fusion.17), kind=kLoop, calls=%fused_computation.6 | loop fusion | flops 4194304 | bytes 16777344 | tf_op jit(solution)/shard_map/jit(_where)/select_n | solution.py:56
  24.6 7.5 %all-to-all-start = ((bf16[16,8,2,2,8,1024]{5,4,3,2,1,0:T(8,128)(2,1)}), bf16[16,8,2,2,8,1024]{5,4,3,2,1,0:T(8,128)(2,1)}, u32[]{:S(2)}, u32[]{:S(2)}) async-start(bf16[16,8,2,2,8,1024]{5,4,3,2,1,0:T(8,128)(2,1)} %broadcast_select_fusion), calls=%async_computation | async-start | bytes 16777216 | tf_op jit(solution)/shard_map/all_to_all | solution.py:61
  32.2 0.3 copy.32
  32.5 0.7 gather_fusion
  33.3 0.1 eq.90
  33.5 0.2 convert_reduce_fusion
  33.8 0.1 broadcast_compare_fusion.1
  34.1 148.7 %all-to-all-done = bf16[16,8,2,2,8,1024]{5,4,3,2,1,0:T(8,128)(2,1)} async-done(((bf16[16,8,2,2,8,1024]{5,4,3,2,1,0:T(8,128)(2,1)}), bf16[16,8,2,2,8,1024]{5,4,3,2,1,0:T(8,128)(2,1)}, u32[]{:S(2)}, u32[]{:S(2)}) %all-to-all-start) | async-done | bytes 8388640 | tf_op jit(solution)/shard_map/all_to_all | solution.py:61
  182.8 6.3 %gather_fusion.3 = bf16[64,2,2,8,1024]{4,3,2,1,0:T(8,128)(2,1)} fusion(bf16[128,2,2,8,1024]{4,3,2,1,0:T(8,128)(2,1)} %bitcast.8, s32[1024]{0:T(1024)S(1)} %pad_clamp_fusion), kind=kCustom, calls=%fused_computation.3 | custom fusion | bytes 8388864 | tf_op jit(solution)/shard_map/gather | solution.py:66
  189.1 2.5 broadcast_select_fusion.1
  191.6 0.6 fusion.29
  192.2 0.6 copy.31
  192.9 0.6 copy.33
  193.5 1.2 fusion.5
  194.7 85.7 %fusion.30 = (f32[64,8,8]{2,1,0:T(8,128)S(1)}, f32[64,8,8,16]{3,2,1,0:T(8,128)S(1)}) fusion(f32[64,8,16,8]{2,3,1,0:T(8,128)S(1)} %fusion.5, pred[64,16]{1,0:T(8,128)(4,1)S(1)} %iota_compare_fusion.1), kind=kOutput, calls=%fused_computation.75 | output fusion | flops 393231 | bytes 541696 | tf_op jit(solution)/shard_map/sub | solution.py:24
  280.4 2.4 multiply_reduce_fusion
  283.1 64.5 %pmax.7 = f32[16]{0:T(128)S(1)} all-reduce(f32[16]{0:T(128)S(1)} %select_reduce_fusion.2), channel_id=1, replica_groups=mesh['groups'=2,'particle'=16] {'particle'}, use_global_device_ids=true, to_apply=%region_9.10 | all-reduce | flops 16 | bytes 128 | tf_op jit(solution)/shard_map/pmax | solution.py:81
  347.6 0.2 exponential_reduce_fusion
  347.8 29.5 %psum.7 = f32[16]{0:T(128)S(1)} all-reduce(f32[16]{0:T(128)S(1)} %exponential_reduce_fusion), channel_id=1, replica_groups=mesh['groups'=2,'particle'=16] {'particle'}, use_global_device_ids=true, to_apply=%region_11.12 | all-reduce | flops 16 | bytes 128 | tf_op jit(solution)/shard_map/psum | solution.py:85
  377.4 0.5 sub.38
  377.9 1.7 copy.44
  379.6 0.3 broadcast_in_dim.119
  379.9 3.9 bitcast_select_fusion
  383.8 2.5 broadcast_in_dim.117
  386.3 19.3 %scatter_fusion = bf16[128,2,8,1024]{3,2,1,0:T(8,128)(2,1)} fusion(bf16[128,2,8,1024]{3,2,1,0:T(8,128)(2,1)} %broadcast_in_dim.117, s32[128]{0:T(128)S(1)} %fusion.22, bf16[128,2,8,1024]{3,2,1,0:T(8,128)(2,1)} %bitcast_select_fusion), kind=kCustom, calls=%fused_computation.4 | custom fusion | bytes 12583424 | tf_op jit(solution)/shard_map/scatter | solution.py:74
  (39 shorter events, 1.3 us)
Async XLA Ops:
  0.6 31.9 %copy-start = (s32[1024]{0:T(1024)S(1)}, s32[1024]{0:T(1024)}, u32[]{:S(2)}) copy-start(s32[1024]{0:T(1024)} %param.9) | copy-start | bytes 12292
  24.6 7.5 %copy-start.4 = (s32[64,2]{0,1:T(2,128)S(1)}, s32[64,2]{0,1:T(2,128)}, u32[]{:S(2)}) copy-start(s32[64,2]{0,1:T(2,128)} %param.8) | copy-start | bytes 1540
  24.6 7.7 %copy-start.3 = (bf16[64,8192]{1,0:T(8,128)(2,1)S(1)}, bf16[64,8192]{1,0:T(8,128)(2,1)}, u32[]{:S(2)}) copy-start(bf16[64,8192]{1,0:T(8,128)(2,1)} %param.11) | copy-start | bytes 3145732
  24.6 158.2 %all-to-all-start = ((bf16[16,8,2,2,8,1024]{5,4,3,2,1,0:T(8,128)(2,1)}), bf16[16,8,2,2,8,1024]{5,4,3,2,1,0:T(8,128)(2,1)}, u32[]{:S(2)}, u32[]{:S(2)}) async-start(bf16[16,8,2,2,8,1024]{5,4,3,2,1,0:T(8,128)(2,1)} %broadcast_select_fusion), calls=%async_computation | async-start | bytes 16777216 | tf_op jit(solution)/shard_map/all_to_all | solution.py:61
  182.8 6.3 %copy-start.2 = (bf16[64,2,1024]{2,1,0:T(2,128)(2,1)S(1)}, bf16[64,2,1024]{2,1,0:T(2,128)(2,1)}, u32[]{:S(2)}) copy-start(bf16[64,2,1024]{2,1,0:T(2,128)(2,1)} %param.12) | copy-start | bytes 786436
  194.7 85.7 %copy-start.5 = (f32[8192]{0:T(1024)S(1)}, f32[8192]{0:T(1024)}, u32[]{:S(2)}) copy-start(f32[8192]{0:T(1024)} %param.13) | copy-start | bytes 98308
  386.3 19.3 %copy-start.1 = (s32[1024]{0:T(1024)S(1)}, s32[1024]{0:T(1024)}, u32[]{:S(2)}) copy-start(s32[1024]{0:T(1024)} %param.9) | copy-start | bytes 12292
where the time goes:
time: 406 us
  waiting for transfers between devices  149 us (37%)
  other arithmetic  102 us (25%)
  blocking collectives  94 us (23%)
  local copies, waits for them, and re-layouts  48.4 us (12%)
  starting transfers between devices  7.53 us (2%)
    all_to_all x1, waiting for transfers between devices, local(): lax.all_to_all(outgoing, 'particle', split_axis=0, concat_axis=0, tiled=T...  149 us
    sub x1, other arithmetic, attend(): expo = jnp.exp(scores - highest)  85.7 us
    pmax x1, blocking collectives, local(): highest = lax.pmax(local_high, 'particle')  64.5 us
    psum x1, blocking collectives, local(): summed = lax.psum(local_sum, 'particle')  29.5 us
    scatter x1, local copies, waits for them, and re-layouts, local(): new_pool = jnp.zeros_like(pool).at[page_table.reshape(-1)].set(descended....  19.3 us
    gather x1, local copies, waits for them, and re-layouts, local(): held_pages[source_row]  8.75 us
  transfers between devices with their start and end apart: 1, of which 1 were waited for; matrix products, arithmetic and copies ran while one was open for 0% of the time, Pallas kernels for 0%

commit v1 on v0

v1 whole, which is shorter than its diff:
```python
import functools

import jax
import jax.numpy as jnp
from jax import lax
from jax.experimental import pallas as pl
from jax.experimental.pallas import tpu as pltpu
from jax.sharding import PartitionSpec as P

HEADS = 64
KV_HEADS = 8
HEAD_DIM = 128
GROUP = 64
BATCH = 8


def pack_kernel(slots, pages, row_ref, table_ref, pool_ref, out_ref, sem):
    def step(j, carry):
        row = row_ref[j]
        for i in range(pages):
            slot = table_ref[row * pages + i]
            pltpu.make_async_copy(pool_ref.at[slot], out_ref.at[j, i], sem).start()
        return carry

    lax.fori_loop(0, slots, step, 0, unroll=4)
    pltpu.make_async_copy(out_ref, out_ref, sem).wait()


def pack(pool, table, source_row, pages):
    slots = source_row.shape[0]
    return pl.pallas_call(
        functools.partial(pack_kernel, slots, pages),
        out_shape=jax.ShapeDtypeStruct((slots, pages) + pool.shape[1:], pool.dtype),
        in_specs=[
            pl.BlockSpec(memory_space=pltpu.SMEM),
            pl.BlockSpec(memory_space=pltpu.SMEM),
            pl.BlockSpec(memory_space=pltpu.VMEM),
        ],
        out_specs=pl.BlockSpec(memory_space=pl.ANY),
        scratch_shapes=[pltpu.SemaphoreType.DMA],
        compiler_params=pltpu.CompilerParams(vmem_limit_bytes=24 << 20),
        name="pack",
    )(source_row, table, pool)


def attend_kernel(
    rows, pages, arrive_ref, table_ref, len_ref,
    held_ref, q_ref, kv_ref, weight_ref,
    pool_ref, attn_ref, part_ref,
    buf, in_sem, out_sem,
):
    page_len = buf.shape[3]
    width = buf.shape[4]
    ctx = pages * page_len

    def fetch(p, carry):
        pltpu.make_async_copy(held_ref.at[arrive_ref[p]], buf.at[p], in_sem.at[p]).start()
        return carry

    lax.fori_loop(0, rows, fetch, 0, unroll=4)

    cols = KV_HEADS * ctx
    head = lax.broadcasted_iota(jnp.int32, (HEADS, cols), 0) // (HEADS // KV_HEADS)
    col = lax.broadcasted_iota(jnp.int32, (HEADS, cols), 1)
    place = jnp.where(head == col // ctx, col % ctx, ctx)
    row = lax.broadcasted_iota(jnp.int32, (page_len, width), 0)

    def step(b, carry):
        p0 = pl.multiple_of(b * BATCH, BATCH)
        fresh = kv_ref[pl.ds(p0, BATCH), :]
        scores = []
        values = []
        for r in range(BATCH):
            p = p0 + r
            pltpu.make_async_copy(held_ref.at[0], buf.at[p], in_sem.at[p]).wait()
            length = len_ref[p]
            cache = []
            for s in range(2):
                new_row = fresh[r:r + 1, s * width:(s + 1) * width]
                now = []
                for i in range(pages):
                    old = buf[p, i, s].astype(jnp.float32)
                    made = jnp.where(row + i * page_len == length, new_row, old)
                    buf[p, i, s] = made.astype(buf.dtype)
                    now.append(made)
                cache.append(jnp.concatenate(
                    [now[i][:, g * HEAD_DIM:(g + 1) * HEAD_DIM] for g in range(KV_HEADS) for i in range(pages)],
                    axis=0,
                ).astype(jnp.bfloat16))
            for i in range(pages):
                slot = table_ref[p * pages + i]
                pltpu.make_async_copy(buf.at[p, i], pool_ref.at[slot], out_sem).start()
            logits = lax.dot_general(
                q_ref[p], cache[0], (((1,), (1,)), ((), ())), preferred_element_type=jnp.float32
            )
            scores.append(jnp.where(place <= length, logits * HEAD_DIM ** (-0.5), -1e30))
            values.append(cache[1])
        weight = weight_ref[...]
        totals = []
        for r in range(BATCH):
            high = jnp.max(scores[r], axis=1, keepdims=True)
            expo = jnp.exp(scores[r] - high)
            probs = (expo / jnp.sum(expo, axis=1, keepdims=True)).astype(jnp.bfloat16)
            mixed = jnp.dot(probs, values[r], preferred_element_type=jnp.float32).astype(attn_ref.dtype)
            attn_ref[p0 + r] = mixed
            totals.append(jnp.sum(mixed.astype(jnp.float32) * weight, axis=0, keepdims=True))
        part_ref[pl.ds(p0, BATCH), :] = jnp.concatenate(totals, axis=0)
        return carry

    lax.fori_loop(0, rows // BATCH, step, 0)
    pltpu.make_async_copy(buf, buf, out_sem).wait()


def attend(held, arrive, table, length_now, query, fresh, weight, pool):
    rows = query.shape[0]
    pages = held.shape[1]
    return pl.pallas_call(
        functools.partial(attend_kernel, rows, pages),
        out_shape=(
            jax.ShapeDtypeStruct(pool.shape, pool.dtype),
            jax.ShapeDtypeStruct(query.shape, jnp.bfloat16),
            jax.ShapeDtypeStruct((rows, HEAD_DIM), jnp.float32),
        ),
        in_specs=[pl.BlockSpec(memory_space=pltpu.SMEM)] * 3
        + [pl.BlockSpec(memory_space=pl.ANY)]
        + [pl.BlockSpec(memory_space=pltpu.VMEM)] * 3,
        out_specs=(
            pl.BlockSpec(memory_space=pl.ANY),
            pl.BlockSpec(memory_space=pltpu.VMEM),
            pl.BlockSpec(memory_space=pltpu.VMEM),
        ),
        scratch_shapes=[
            pltpu.VMEM((rows,) + held.shape[1:], held.dtype),
            pltpu.SemaphoreType.DMA((rows,)),
            pltpu.SemaphoreType.DMA,
        ],
        compiler_params=pltpu.CompilerParams(vmem_limit_bytes=32 << 20),
        name="attend",
    )(arrive, table, length_now, held, query, fresh, weight)


def spread_kernel(devices, mine_ref, all_ref, landed, send_sem, recv_sem):
    me = lax.axis_index("particle")
    barrier = pltpu.get_barrier_semaphore()

    def greet(k, carry):
        pl.semaphore_signal(
            barrier, inc=1, device_id={"particle": lax.rem(me + k, devices)},
            device_id_type=pl.DeviceIdType.MESH,
        )
        return carry

    lax.fori_loop(1, devices, greet, 0)
    pl.semaphore_wait(barrier, devices - 1)

    def copy_to(k):
        return pltpu.make_async_remote_copy(
            src_ref=mine_ref,
            dst_ref=landed.at[k],
            send_sem=send_sem.at[k],
            recv_sem=recv_sem.at[k],
            device_id={"particle": lax.rem(me + k, devices)},
            device_id_type=pl.DeviceIdType.MESH,
        )

    def send(k, carry):
        copy_to(k).start()
        return carry

    def finish(k, carry):
        copy_to(k).wait()
        return carry

    lax.fori_loop(1, devices, send, 0)
    landed[0] = mine_ref[...]
    lax.fori_loop(1, devices, finish, 0)
    all_ref[...] = landed[...]


def spread(mine, devices):
    return pl.pallas_call(
        functools.partial(spread_kernel, devices),
        out_shape=jax.ShapeDtypeStruct((devices,) + mine.shape, mine.dtype),
        in_specs=[pl.BlockSpec(memory_space=pltpu.VMEM)],
        out_specs=pl.BlockSpec(memory_space=pltpu.VMEM),
        scratch_shapes=[
            pltpu.VMEM((devices,) + mine.shape, mine.dtype),
            pltpu.SemaphoreType.DMA((devices,)),
            pltpu.SemaphoreType.DMA((devices,)),
        ],
        compiler_params=pltpu.CompilerParams(collective_id=0, has_side_effects=True),
        name="spread",
    )(mine)


def local(pool, page_table, lengths, ancestors, new_q, new_kv, score_weight):
    devices = lax.axis_size("particle")
    self_index = lax.axis_index("particle")
    per_device = new_q.shape[0]
    page_count = page_table.shape[1]
    prompts = devices * per_device // GROUP
    stride = max(1, prompts // per_device)
    reach_size = devices // stride
    capacity = 2 * per_device // reach_size
    table = page_table.reshape(-1)
    anc_all = ancestors.reshape(devices, per_device)
    anc_dev = anc_all // per_device
    row_order = jnp.arange(per_device, dtype=jnp.int32)
    my_ancestors = lax.dynamic_slice_in_dim(anc_all, self_index, 1, 0)[0]
    my_sources = my_ancestors // per_device
    from_self = anc_dev == self_index
    slot_rank = jnp.cumsum(from_self.astype(jnp.int32), axis=1) - 1
    picked = from_self[:, None, :] & (
        slot_rank[:, None, :] == jnp.arange(capacity, dtype=jnp.int32)[None, :, None]
    )
    source_row = jnp.sum(jnp.where(picked, anc_all[:, None, :] % per_device, 0), axis=2)
    outgoing = pack(pool, table, source_row.reshape(-1), page_count)
    outgoing = outgoing.reshape((devices, capacity) + outgoing.shape[1:])
    incoming = lax.all_to_all(outgoing, "particle", split_axis=0, concat_axis=0, tiled=True)
    incoming = incoming.reshape((devices * capacity,) + incoming.shape[2:])
    earlier = (my_sources[None, :] == my_sources[:, None]) & (
        row_order[None, :] < row_order[:, None]
    )
    arrive_slot = my_sources * capacity + jnp.sum(earlier.astype(jnp.int32), axis=1)
    length_now = lengths[my_ancestors]
    new_pool, attn_out, partial_sums = attend(
        incoming, arrive_slot, table, length_now,
        new_q.reshape(per_device, HEADS, HEAD_DIM),
        new_kv.astype(jnp.float32).reshape(per_device, -1),
        score_weight.reshape(HEADS, HEAD_DIM), pool,
    )
    attn_out = attn_out.reshape(new_q.shape)
    reward = jnp.sum(partial_sums, axis=1)
    mine = jnp.broadcast_to(reward[None, :], (8, per_device))
    mine = jnp.pad(mine, ((0, 0), (0, (-per_device) % 128)))
    landed = spread(mine, devices)[:, 0, :per_device]
    owner = (self_index - jnp.arange(devices, dtype=jnp.int32)) % devices
    landed_prompt = (owner[:, None] * per_device + row_order[None, :]) % prompts
    my_prompt = (self_index * per_device + row_order) % prompts
    member = landed_prompt.reshape(-1)[None, :] == my_prompt[:, None]
    rewards = landed.reshape(-1)[None, :]
    highest = jnp.max(jnp.where(member, rewards, -jnp.inf), axis=1)
    summed = jnp.sum(jnp.exp(jnp.where(member, rewards - highest[:, None], -jnp.inf)), axis=1)
    log_weights = reward - (highest + jnp.log(summed))
    return (new_pool, attn_out, log_weights)


def solution(mesh):
    in_specs = (
        P(("groups", "particle"), None, None, None),
        P(("groups", "particle"), None),
        P("groups"),
        P("groups"),
        P(("groups", "particle"), None),
        P(("groups", "particle"), None, None),
        P(),
    )
    out_specs = (
        P(("groups", "particle"), None, None, None),
        P(("groups", "particle"), None),
        P(("groups", "particle")),
    )
    return jax.shard_map(local, mesh=mesh, in_specs=in_specs, out_specs=out_specs, check_vma=False)
```

time: 406 us -> 240 us (0.59)
  other arithmetic: 102 us -> 2 us
  blocking collectives: 94 us -> 0 us
  Pallas kernels: 0 us -> 68.5 us
  local copies, waits for them, and re-layouts: 48.4 us -> 11.5 us
    sub x2 -> x1, other arithmetic: 86.2 us -> 0.53 us  [local(): log_weights = reward - (highest + jnp.log(summed))]
    pallas_call x0 -> x3, Pallas kernels: none -> 68.5 us  [the longest x1 40.2 us: spread(): pl.pallas_call(functools.partial(spread_kernel, devices), out_shape=jax.S...]
    pmax x1 -> x0, blocking collectives: 64.5 us -> none  [local(): highest = lax.pmax(local_high, 'particle')]
    psum x1 -> x0, blocking collectives: 29.5 us -> none  [local(): summed = lax.psum(local_sum, 'particle')]
    gather x3 -> x0, local copies, waits for them, and re-layouts: 20 us -> none  [the longest x1 8.75 us: local(): held_pages[source_row]]
    scatter x1 -> x0, local copies, waits for them, and re-layouts: 19.3 us -> none  [local(): new_pool = jnp.zeros_like(pool).at[page_table.reshape(-1)].set(descended....]
    select_n x8 -> x3, other arithmetic: 14.4 us -> 0.04 us  [the longest x1 0.02 us: local(): my_sources = my_ancestors // per_device]
    unnamed x17 -> x16, local copies, waits for them, and re-layouts: 3.33 us -> 8.19 us
  transfers between devices with their start and end apart: 1 -> 1, of which waited for: 1 -> 1; matrix products, arithmetic and copies ran while one was open for 0% -> 1% of each run, Pallas kernels for 0% -> 0%
where the time goes in v1:
time: 240 us
  waiting for transfers between devices  149 us (62%)
  Pallas kernels  68.5 us (29%)
  local copies, waits for them, and re-layouts  11.5 us (5%)
  starting transfers between devices  7.57 us (3%)
    all_to_all x1, waiting for transfers between devices, local(): lax.all_to_all(outgoing, 'particle', split_axis=0, concat_axis=0, tiled=T...  149 us
    pallas_call x1, Pallas kernels, spread(): pl.pallas_call(functools.partial(spread_kernel, devices), out_shape=jax.S...  40.2 us
    pallas_call x1, Pallas kernels, attend(): pl.pallas_call(functools.partial(attend_kernel, rows, pages), out_shape=(...  15.2 us
    pallas_call x1, Pallas kernels, pack(): pl.pallas_call(functools.partial(pack_kernel, slots, pages), out_shape=ja...  13 us
    unnamed x16, local copies, waits for them, and re-layouts  8.19 us
    all_to_all x1, starting transfers between devices, local(): lax.all_to_all(outgoing, 'particle', split_axis=0, concat_axis=0, tiled=T...  7.57 us
  transfers between devices with their start and end apart: 1, of which 1 were waited for; matrix products, arithmetic and copies ran while one was open for 1% of the time, Pallas kernels for 0%

profile of v1, /device:TPU:0, one launch (start us, length us, event | category | flops | bytes accessed | tf_op | source)
XLA Modules:
  0.0 239.5 jit_solution(3748297156512945908)
XLA Ops:
  0.6 0.0 copy-start
  0.6 0.8 reshape.242
  1.4 0.8 copy.12
  2.2 0.1 reshape.243.table_ref
  2.3 0.2 reduce_window_sum.11
  2.6 0.3 select_reduce_fusion
  2.9 0.1 reshape.244.row_ref
  3.0 0.0 copy-start.2
  3.0 2.2 copy-done.2
  5.2 13.0 %pack.1 = bf16[128,2,2,8,1024]{4,3,2,1,0:T(8,128)(2,1)S(1)} custom-call(s32[128]{0:T(128)S(1)} %reshape.244.row_ref, s32[128]{0:T(128)S(1)} %reshape.243.table_ref, bf16[128,2,8,1024]{3,2,1,0:T(8,128)(2,1)S(1)} %copy-done.2), custom_call_target="tpu_custom_call" | custom-call | tf_op jit(solution)/shard_map/pack/pallas_call | solution.py:31
  18.2 0.0 copy-start.1
  18.2 3.2 %copy-done.1 = bf16[128,2,2,8,1024]{4,3,2,1,0:T(8,128)(2,1)} copy-done((bf16[128,2,2,8,1024]{4,3,2,1,0:T(8,128)(2,1)}, bf16[128,2,2,8,1024]{4,3,2,1,0:T(8,128)(2,1)S(1)}, u32[]{:S(2)}) %copy-start.1) | copy-done | bytes 8388632
  21.4 7.6 %all-to-all-start = ((bf16[16,8,2,2,8,1024]{5,4,3,2,1,0:T(8,128)(2,1)}), bf16[16,8,2,2,8,1024]{5,4,3,2,1,0:T(8,128)(2,1)}, u32[]{:S(2)}, u32[]{:S(2)}) async-start(bf16[16,8,2,2,8,1024]{5,4,3,2,1,0:T(8,128)(2,1)} %bitcast.28), calls=%async_computation | async-start | bytes 16777216 | tf_op jit(solution)/shard_map/all_to_all | solution.py:219
  29.0 0.3 copy.13
  29.3 0.1 copy.14
  29.4 0.1 iota_add_fusion
  29.5 0.1 add.124
  29.6 0.0 copy-done
  29.6 0.7 gather_fusion
  30.4 0.2 convert_reduce_fusion
  30.6 149.2 %all-to-all-done = bf16[16,8,2,2,8,1024]{5,4,3,2,1,0:T(8,128)(2,1)} async-done(((bf16[16,8,2,2,8,1024]{5,4,3,2,1,0:T(8,128)(2,1)}), bf16[16,8,2,2,8,1024]{5,4,3,2,1,0:T(8,128)(2,1)}, u32[]{:S(2)}, u32[]{:S(2)}) %all-to-all-start) | async-done | bytes 8388640 | tf_op jit(solution)/shard_map/all_to_all | solution.py:219
  179.7 0.0 copy-done.3
  179.7 15.2 %attend.1 = (bf16[128,2,8,1024]{3,2,1,0:T(8,128)(2,1)}, bf16[64,64,128]{2,1,0:T(8,128)(2,1)S(1)}, f32[64,128]{1,0:T(8,128)S(1)}) custom-call(s32[64]{0:T(128)S(1)} %multiply_add_fusion.arrive_ref, s32[128]{0:T(128)S(1)} %reshape.243.table_ref, s32[64]{0:T(128)S(1)} %gather_fusion, bf16[128,2,2,8,1024]{4,3,2,1,0:T(8,128)(2,1)} %bitcast.5.held_ref, ...), custom_call_target="tpu_custom_call" | custom-call | tf_op jit(solution)/shard_map/attend/pallas_call | solution.py:117
  195.0 1.7 copy.17
  196.7 0.1 reduce_sum.38
  196.8 0.6 pad.7.mine_ref
  197.4 40.2 %spread.1 = f32[16,8,128]{2,1,0:T(8,128)} custom-call(f32[8,128]{1,0:T(8,128)} %pad.7.mine_ref), custom_call_target="tpu_custom_call" | custom-call | tf_op jit(solution)/shard_map/spread/pallas_call | solution.py:181
  237.6 0.9 slice_reduce_fusion
  238.5 0.1 broadcast_in_dim.25
  238.6 0.2 fusion
  238.8 0.2 fusion.2
  239.0 0.5 add_subtract_fusion
  (16 shorter events, 0.1 us)
Async XLA Ops:
  0.6 28.9 %copy-start = (s32[1024]{0:T(1024)S(1)}, s32[1024]{0:T(1024)}, u32[]{:S(2)}) copy-start(s32[1024]{0:T(1024)} %param.9) | copy-start | bytes 12292
  3.0 2.2 copy-start.2
  18.2 3.2 %copy-start.1 = (bf16[128,2,2,8,1024]{4,3,2,1,0:T(8,128)(2,1)}, bf16[128,2,2,8,1024]{4,3,2,1,0:T(8,128)(2,1)S(1)}, u32[]{:S(2)}) copy-start(bf16[128,2,2,8,1024]{4,3,2,1,0:T(8,128)(2,1)S(1)} %pack.1) | copy-start | bytes 25165828
  21.4 7.6 %copy-start.4 = (bf16[64,8192]{1,0:T(8,128)(2,1)S(1)}, bf16[64,8192]{1,0:T(8,128)(2,1)}, u32[]{:S(2)}) copy-start(bf16[64,8192]{1,0:T(8,128)(2,1)} %param.11) | copy-start | bytes 3145732
  21.4 7.9 %copy-start.5 = (bf16[64,2,1024]{2,1,0:T(2,128)(2,1)S(1)}, bf16[64,2,1024]{2,1,0:T(2,128)(2,1)}, u32[]{:S(2)}) copy-start(bf16[64,2,1024]{2,1,0:T(2,128)(2,1)} %param.12) | copy-start | bytes 786436
  21.4 158.3 %copy-start.3 = (f32[8192]{0:T(1024)S(1)}, f32[8192]{0:T(1024)}, u32[]{:S(2)}) copy-start(f32[8192]{0:T(1024)} %param.13) | copy-start | bytes 98308
  21.4 158.3 %all-to-all-start = ((bf16[16,8,2,2,8,1024]{5,4,3,2,1,0:T(8,128)(2,1)}), bf16[16,8,2,2,8,1024]{5,4,3,2,1,0:T(8,128)(2,1)}, u32[]{:S(2)}, u32[]{:S(2)}) async-start(bf16[16,8,2,2,8,1024]{5,4,3,2,1,0:T(8,128)(2,1)} %bitcast.28), calls=%async_computation | async-start | bytes 16777216 | tf_op jit(solution)/shard_map/all_to_all | solution.py:219

commit v2 on v1

--- a/solution.py
+++ b/solution.py
@@ -14,33 +14,94 @@
 BATCH = 8
 
 
-def pack_kernel(slots, pages, row_ref, table_ref, pool_ref, out_ref, sem):
-    def step(j, carry):
-        row = row_ref[j]
-        for i in range(pages):
-            slot = table_ref[row * pages + i]
-            pltpu.make_async_copy(pool_ref.at[slot], out_ref.at[j, i], sem).start()
-        return carry
-
-    lax.fori_loop(0, slots, step, 0, unroll=4)
-    pltpu.make_async_copy(out_ref, out_ref, sem).wait()
-
-
-def pack(pool, table, source_row, pages):
-    slots = source_row.shape[0]
+def exchange_kernel(
+    devices, capacity, pages, row_ref, table_ref, pool_ref, held_ref,
+    stage, send_sem, recv_sem, own_sem,
+):
+    me = lax.axis_index("particle")
+    barrier = pltpu.get_barrier_semaphore()
+
+    def greet(k, carry):
+        pl.semaphore_signal(
+            barrier, inc=1, device_id={"particle": lax.rem(me + k, devices)},
+            device_id_type=pl.DeviceIdType.MESH,
+        )
+        return carry
+
+    lax.fori_loop(1, devices, greet, 0)
+
+    def fill(k):
+        base = lax.rem(me + k, devices) * capacity
+        for c in range(capacity):
+            row = row_ref[base + c]
+            for i in range(pages):
+                stage[k, c, i] = pool_ref[table_ref[row * pages + i]]
+
+    def copy_to(k):
+        return pltpu.make_async_remote_copy(
+            src_ref=stage.at[k],
+            dst_ref=held_ref.at[me],
+            send_sem=send_sem.at[k],
+            recv_sem=recv_sem.at[k],
+            device_id={"particle": lax.rem(me + k, devices)},
+            device_id_type=pl.DeviceIdType.MESH,
+        )
+
+    def send(i, carry):
+        half = i // 2
+        odd = half % 2
+        step = (half + 1) // 2
+        far = devices // 2 + step - 2 * step * odd
+        near = (1 - odd) * (devices - 1 - half // 2) + odd * (1 + half // 2)
+        k = far + (i % 2) * (near - far)
+        fill(k)
+        copy_to(k).start()
+        return carry
+
+    def finish(k, carry):
+        source = lax.rem(me + devices - k, devices)
+        pltpu.make_async_remote_copy(
+            src_ref=stage.at[k],
+            dst_ref=held_ref.at[source],
+            send_sem=send_sem.at[k],
+            recv_sem=recv_sem.at[k],
+            device_id={"particle": lax.rem(me + k, devices)},
+            device_id_type=pl.DeviceIdType.MESH,
+        ).wait()
+        return carry
+
+    pl.semaphore_wait(barrier, devices - 1)
+    lax.fori_loop(0, devices - 1, send, 0)
+    fill(0)
+    own = pltpu.make_async_copy(stage.at[0], held_ref.at[me], own_sem)
+    own.start()
+    lax.fori_loop(1, devices, finish, 0)
+    own.wait()
+
+
+def exchange(pool, table, source_row, pages):
+    devices, capacity = source_row.shape
+    block = (capacity, pages) + pool.shape[1:]
     return pl.pallas_call(
-        functools.partial(pack_kernel, slots, pages),
-        out_shape=jax.ShapeDtypeStruct((slots, pages) + pool.shape[1:], pool.dtype),
+        functools.partial(exchange_kernel, devices, capacity, pages),
+        out_shape=jax.ShapeDtypeStruct((devices,) + block, pool.dtype),
         in_specs=[
             pl.BlockSpec(memory_space=pltpu.SMEM),
             pl.BlockSpec(memory_space=pltpu.SMEM),
             pl.BlockSpec(memory_space=pltpu.VMEM),
         ],
         out_specs=pl.BlockSpec(memory_space=pl.ANY),
-        scratch_shapes=[pltpu.SemaphoreType.DMA],
-        compiler_params=pltpu.CompilerParams(vmem_limit_bytes=24 << 20),
-        name="pack",
-    )(source_row, table, pool)
+        scratch_shapes=[
+            pltpu.VMEM((devices,) + block, pool.dtype),
+            pltpu.SemaphoreType.DMA((devices,)),
+            pltpu.SemaphoreType.DMA((devices,)),
+            pltpu.SemaphoreType.DMA,
+        ],
+        compiler_params=pltpu.CompilerParams(
+            collective_id=1, has_side_effects=True, vmem_limit_bytes=40 << 20
+        ),
+        name="exchange",
+    )(source_row.reshape(-1), table, pool)
 
 
 def attend_kernel(
@@ -214,9 +275,7 @@
         slot_rank[:, None, :] == jnp.arange(capacity, dtype=jnp.int32)[None, :, None]
     )
     source_row = jnp.sum(jnp.where(picked, anc_all[:, None, :] % per_device, 0), axis=2)
-    outgoing = pack(pool, table, source_row.reshape(-1), page_count)
-    outgoing = outgoing.reshape((devices, capacity) + outgoing.shape[1:])
-    incoming = lax.all_to_all(outgoing, "particle", split_axis=0, concat_axis=0, tiled=True)
+    incoming = exchange(pool, table, source_row, page_count)
     incoming = incoming.reshape((devices * capacity,) + incoming.shape[2:])
     earlier = (my_sources[None, :] == my_sources[:, None]) & (
         row_order[None, :] < row_order[:, None]

time: 240 us -> 234 us (0.975)
  waiting for transfers between devices: 149 us -> 0 us
  Pallas kernels: 68.5 us -> 216 us
  starting transfers between devices: 7.57 us -> 0 us
  local copies, waits for them, and re-layouts: 11.5 us -> 14.9 us
    pallas_call x1, Pallas kernels: 13 us -> 166 us  [exchange(): pl.pallas_call(functools.partial(exchange_kernel, devices, capacity, page...]
    all_to_all x1 -> x0, waiting for transfers between devices: 149 us -> none  [local(): lax.all_to_all(outgoing, 'particle', split_axis=0, concat_axis=0, tiled=T...]
    pallas_call x1, Pallas kernels: 40.2 us -> 29.7 us  [spread(): pl.pallas_call(functools.partial(spread_kernel, devices), out_shape=jax.S...]
    all_to_all x1 -> x0, starting transfers between devices: 7.57 us -> none  [local(): lax.all_to_all(outgoing, 'particle', split_axis=0, concat_axis=0, tiled=T...]
    pallas_call x1, Pallas kernels: 15.2 us -> 20.1 us  [attend(): pl.pallas_call(functools.partial(attend_kernel, rows, pages), out_shape=(...]
    unnamed x16 -> x18, local copies, waits for them, and re-layouts: 8.19 us -> 11.6 us
  transfers between devices with their start and end apart: 1 -> 0, of which waited for: 1 -> 0; matrix products, arithmetic and copies ran while one was open for 1% -> 0% of each run, Pallas kernels for 0% -> 0%
where the time goes in v2:
time: 234 us; the launch traced here: 233 us
  Pallas kernels  216 us (92%)
  local copies, waits for them, and re-layouts  14.9 us (6%)
    pallas_call x1, Pallas kernels, exchange(): pl.pallas_call(functools.partial(exchange_kernel, devices, capacity, page...  166 us
    pallas_call x1, Pallas kernels, spread(): pl.pallas_call(functools.partial(spread_kernel, devices), out_shape=jax.S...  29.7 us
    pallas_call x1, Pallas kernels, attend(): pl.pallas_call(functools.partial(attend_kernel, rows, pages), out_shape=(...  20.1 us
    unnamed x18, local copies, waits for them, and re-layouts  11.6 us

profile of v2, /device:TPU:0, one launch (start us, length us, event | category | flops | bytes accessed | tf_op | source)
XLA Modules:
  0.0 233.3 jit_solution(9298252116136309129)
XLA Ops:
  0.6 0.0 copy-start
  0.6 0.8 reshape.239
  1.4 0.2 convert_reduce_fusion
  1.7 0.2 reduce_window_sum.11
  1.9 0.3 select_reduce_fusion
  2.2 0.1 reshape.241.row_ref
  2.3 0.8 copy.12
  3.1 0.1 reshape.240.table_ref
  3.3 0.0 copy-start.3
  3.3 2.2 copy-done.3
  5.5 165.8 %exchange.1 = bf16[16,8,2,2,8,1024]{5,4,3,2,1,0:T(8,128)(2,1)S(1)} custom-call(s32[128]{0:T(128)S(1)} %reshape.241.row_ref, s32[128]{0:T(128)S(1)} %reshape.240.table_ref, bf16[128,2,8,1024]{3,2,1,0:T(8,128)(2,1)S(1)} %copy-done.3), custom_call_target="tpu_custom_call" | custom-call | tf_op jit(solution)/shard_map/exchange/pallas_call | solution.py:85
  171.2 0.0 copy-start.1
  171.2 3.2 %copy-done.1 = bf16[16,8,2,2,8,1024]{5,4,3,2,1,0:T(8,128)(2,1)} copy-done((bf16[16,8,2,2,8,1024]{5,4,3,2,1,0:T(8,128)(2,1)}, bf16[16,8,2,2,8,1024]{5,4,3,2,1,0:T(8,128)(2,1)S(1)}, u32[]{:S(2)}) %copy-start.1) | copy-done | bytes 8388632
  174.5 0.0 copy-done
  174.5 0.7 gather_fusion
  175.2 0.0 copy-done.5
  175.2 0.3 copy.13
  175.5 0.0 copy-done.6
  175.5 0.1 copy.14
  175.6 3.4 %copy-done.2 = bf16[16,8,2,2,8,1024]{5,4,3,2,1,0:T(8,128)(2,1)S(1)} copy-done((bf16[16,8,2,2,8,1024]{5,4,3,2,1,0:T(8,128)(2,1)S(1)}, bf16[16,8,2,2,8,1024]{5,4,3,2,1,0:T(8,128)(2,1)}, u32[]{:S(2)}) %copy-start.2) | copy-done | bytes 8388632
  178.9 20.1 %attend.1 = (bf16[128,2,8,1024]{3,2,1,0:T(8,128)(2,1)}, bf16[64,64,128]{2,1,0:T(8,128)(2,1)S(1)}, f32[64,128]{1,0:T(8,128)S(1)}) custom-call(s32[64]{0:T(128)S(1)} %multiply_add_fusion.arrive_ref, s32[128]{0:T(128)S(1)} %reshape.240.table_ref, s32[64]{0:T(128)S(1)} %gather_fusion, bf16[128,2,2,8,1024]{4,3,2,1,0:T(8,128)(2,1)S(1)} %bitcast.27, ...), custom_call_target="tpu_custom_call" | custom-call | tf_op jit(solution)/shard_map/attend/pallas_call | solution.py:178
  199.1 0.1 reduce_sum.38
  199.2 0.6 pad.7.mine_ref
  199.8 29.7 %spread.1 = f32[16,8,128]{2,1,0:T(8,128)} custom-call(f32[8,128]{1,0:T(8,128)} %pad.7.mine_ref), custom_call_target="tpu_custom_call" | custom-call | tf_op jit(solution)/shard_map/spread/pallas_call | solution.py:242
  229.5 0.9 slice_reduce_fusion
  230.4 0.1 broadcast_in_dim.25
  230.5 0.1 iota_add_fusion
  230.6 0.1 add.124
  230.7 0.2 fusion
  230.9 0.2 fusion.2
  231.1 0.5 add_subtract_fusion
  231.6 1.7 copy.17
  (16 shorter events, 0.1 us)
Async XLA Ops:
  0.6 173.8 %copy-start = (s32[1024]{0:T(1024)S(1)}, s32[1024]{0:T(1024)}, u32[]{:S(2)}) copy-start(s32[1024]{0:T(1024)} %param.9) | copy-start | bytes 12292
  3.3 2.2 copy-start.3
  5.5 169.7 %copy-start.5 = (bf16[64,8192]{1,0:T(8,128)(2,1)S(1)}, bf16[64,8192]{1,0:T(8,128)(2,1)}, u32[]{:S(2)}) copy-start(bf16[64,8192]{1,0:T(8,128)(2,1)} %param.11) | copy-start | bytes 3145732
  5.5 170.0 %copy-start.6 = (bf16[64,2,1024]{2,1,0:T(2,128)(2,1)S(1)}, bf16[64,2,1024]{2,1,0:T(2,128)(2,1)}, u32[]{:S(2)}) copy-start(bf16[64,2,1024]{2,1,0:T(2,128)(2,1)} %param.12) | copy-start | bytes 786436
  5.5 170.1 %copy-start.4 = (f32[8192]{0:T(1024)S(1)}, f32[8192]{0:T(1024)}, u32[]{:S(2)}) copy-start(f32[8192]{0:T(1024)} %param.13) | copy-start | bytes 98308
  171.2 3.2 %copy-start.1 = (bf16[16,8,2,2,8,1024]{5,4,3,2,1,0:T(8,128)(2,1)}, bf16[16,8,2,2,8,1024]{5,4,3,2,1,0:T(8,128)(2,1)S(1)}, u32[]{:S(2)}) copy-start(bf16[16,8,2,2,8,1024]{5,4,3,2,1,0:T(8,128)(2,1)S(1)} %exchange.1) | copy-start | bytes 25165828
  175.6 3.4 %copy-start.2 = (bf16[16,8,2,2,8,1024]{5,4,3,2,1,0:T(8,128)(2,1)S(1)}, bf16[16,8,2,2,8,1024]{5,4,3,2,1,0:T(8,128)(2,1)}, u32[]{:S(2)}) copy-start(bf16[16,8,2,2,8,1024]{5,4,3,2,1,0:T(8,128)(2,1)} %copy-done.1) | copy-start | bytes 25165828

commit v3 on v2

--- a/solution.py
+++ b/solution.py
@@ -11,7 +11,7 @@
 KV_HEADS = 8
 HEAD_DIM = 128
 GROUP = 64
-BATCH = 8
+BATCH = 16
 
 
 def exchange_kernel(
@@ -90,7 +90,7 @@
             pl.BlockSpec(memory_space=pltpu.SMEM),
             pl.BlockSpec(memory_space=pltpu.VMEM),
         ],
-        out_specs=pl.BlockSpec(memory_space=pl.ANY),
+        out_specs=pl.BlockSpec(memory_space=pltpu.HBM),
         scratch_shapes=[
             pltpu.VMEM((devices,) + block, pool.dtype),
             pltpu.SemaphoreType.DMA((devices,)),
@@ -98,7 +98,7 @@
             pltpu.SemaphoreType.DMA,
         ],
         compiler_params=pltpu.CompilerParams(
-            collective_id=1, has_side_effects=True, vmem_limit_bytes=40 << 20
+            collective_id=1, has_side_effects=True, vmem_limit_bytes=48 << 20
         ),
         name="exchange",
     )(source_row.reshape(-1), table, pool)
@@ -183,7 +183,7 @@
             jax.ShapeDtypeStruct((rows, HEAD_DIM), jnp.float32),
         ),
         in_specs=[pl.BlockSpec(memory_space=pltpu.SMEM)] * 3
-        + [pl.BlockSpec(memory_space=pl.ANY)]
+        + [pl.BlockSpec(memory_space=pltpu.HBM)]
         + [pl.BlockSpec(memory_space=pltpu.VMEM)] * 3,
         out_specs=(
             pl.BlockSpec(memory_space=pl.ANY),
@@ -200,8 +200,10 @@
     )(arrive, table, length_now, held, query, fresh, weight)
 
 
-def spread_kernel(devices, mine_ref, all_ref, landed, send_sem, recv_sem):
+def weights_kernel(devices, prompts, part_ref, out_ref, mine, landed, send_sem, recv_sem):
     me = lax.axis_index("particle")
+    rows = part_ref.shape[0]
+    lanes = out_ref.shape[1]
     barrier = pltpu.get_barrier_semaphore()
 
     def greet(k, carry):
@@ -212,11 +214,15 @@
         return carry
 
     lax.fori_loop(1, devices, greet, 0)
+    reward = jnp.sum(part_ref[...].T, axis=0, keepdims=True)
+    reward = jnp.concatenate([reward] * (lanes // rows), axis=1)
+    reward = jnp.broadcast_to(reward, out_ref.shape)
+    mine[...] = reward
     pl.semaphore_wait(barrier, devices - 1)
 
     def copy_to(k):
         return pltpu.make_async_remote_copy(
-            src_ref=mine_ref,
+            src_ref=mine,
             dst_ref=landed.at[k],
             send_sem=send_sem.at[k],
             recv_sem=recv_sem.at[k],
@@ -233,25 +239,39 @@
         return carry
 
     lax.fori_loop(1, devices, send, 0)
-    landed[0] = mine_ref[...]
     lax.fori_loop(1, devices, finish, 0)
-    all_ref[...] = landed[...]
-
-
-def spread(mine, devices):
+    stride = max(1, prompts // rows)
+    table = [reward] + [landed[k] for k in range(stride, devices, stride)]
+    shifts = []
+    shift = prompts
+    while shift < rows:
+        shifts.append(shift)
+        shift *= 2
+    high = functools.reduce(jnp.maximum, table)
+    for shift in shifts:
+        high = jnp.maximum(high, pltpu.roll(high, shift, 1))
+    total = sum(jnp.exp(entry - high) for entry in table)
+    for shift in shifts:
+        total = total + pltpu.roll(total, shift, 1)
+    out_ref[...] = reward - (high + jnp.log(total))
+
+
+def weights(partial_sums, devices, prompts):
+    tile = (8, 128)
     return pl.pallas_call(
-        functools.partial(spread_kernel, devices),
-        out_shape=jax.ShapeDtypeStruct((devices,) + mine.shape, mine.dtype),
+        functools.partial(weights_kernel, devices, prompts),
+        out_shape=jax.ShapeDtypeStruct(tile, jnp.float32),
         in_specs=[pl.BlockSpec(memory_space=pltpu.VMEM)],
         out_specs=pl.BlockSpec(memory_space=pltpu.VMEM),
         scratch_shapes=[
-            pltpu.VMEM((devices,) + mine.shape, mine.dtype),
+            pltpu.VMEM(tile, jnp.float32),
+            pltpu.VMEM((devices,) + tile, jnp.float32),
             pltpu.SemaphoreType.DMA((devices,)),
             pltpu.SemaphoreType.DMA((devices,)),
         ],
         compiler_params=pltpu.CompilerParams(collective_id=0, has_side_effects=True),
-        name="spread",
-    )(mine)
+        name="weights",
+    )(partial_sums)
 
 
 def local(pool, page_table, lengths, ancestors, new_q, new_kv, score_weight):
@@ -289,18 +309,7 @@
         score_weight.reshape(HEADS, HEAD_DIM), pool,
     )
     attn_out = attn_out.reshape(new_q.shape)
-    reward = jnp.sum(partial_sums, axis=1)
-    mine = jnp.broadcast_to(reward[None, :], (8, per_device))
-    mine = jnp.pad(mine, ((0, 0), (0, (-per_device) % 128)))
-    landed = spread(mine, devices)[:, 0, :per_device]
-    owner = (self_index - jnp.arange(devices, dtype=jnp.int32)) % devices
-    landed_prompt = (owner[:, None] * per_device + row_order[None, :]) % prompts
-    my_prompt = (self_index * per_device + row_order) % prompts
-    member = landed_prompt.reshape(-1)[None, :] == my_prompt[:, None]
-    rewards = landed.reshape(-1)[None, :]
-    highest = jnp.max(jnp.where(member, rewards, -jnp.inf), axis=1)
-    summed = jnp.sum(jnp.exp(jnp.where(member, rewards - highest[:, None], -jnp.inf)), axis=1)
-    log_weights = reward - (highest + jnp.log(summed))
+    log_weights = weights(partial_sums, devices, prompts)[0, :per_device]
     return (new_pool, attn_out, log_weights)
 
 

time: 234 us -> 231 us (0.987)
    unnamed x18 -> x14, local copies, waits for them, and re-layouts: 11.6 us -> 10.6 us
where the time goes in v3:
time: 231 us; the launch traced here: 230 us
  Pallas kernels  215 us (93%)
  local copies, waits for them, and re-layouts  13.4 us (6%)
    pallas_call x1, Pallas kernels, exchange(): pl.pallas_call(functools.partial(exchange_kernel, devices, capacity, page...  166 us
    pallas_call x1, Pallas kernels, weights(): pl.pallas_call(functools.partial(weights_kernel, devices, prompts), out_s...  30.1 us
    pallas_call x1, Pallas kernels, attend(): pl.pallas_call(functools.partial(attend_kernel, rows, pages), out_shape=(...  19.2 us
    unnamed x14, local copies, waits for them, and re-layouts  10.6 us

profile of v3, /device:TPU:0, one launch (start us, length us, event | category | flops | bytes accessed | tf_op | source)
XLA Modules:
  0.0 230.2 jit_solution(13491232645280817570)
XLA Ops:
  0.6 0.0 copy-start
  0.6 0.8 reshape.179
  1.5 0.2 convert_reduce_fusion
  1.7 0.0 copy-done
  1.7 0.7 gather_fusion
  2.4 0.2 reduce_window_sum.11
  2.7 0.3 select_reduce_fusion
  3.0 0.1 reshape.181.row_ref
  3.1 0.8 copy.12
  3.9 0.1 reshape.180.table_ref
  4.0 1.0 copy.14
  5.0 1.5 copy.13
  6.5 0.0 copy-start.2
  6.6 2.2 copy-done.2
  8.7 0.0 copy-start.3
  8.7 165.9 %exchange.1 = bf16[16,8,2,2,8,1024]{5,4,3,2,1,0:T(8,128)(2,1)} custom-call(s32[128]{0:T(128)S(1)} %reshape.181.row_ref, s32[128]{0:T(128)S(1)} %reshape.180.table_ref, bf16[128,2,8,1024]{3,2,1,0:T(8,128)(2,1)S(1)} %copy-done.2), custom_call_target="tpu_custom_call" | custom-call | tf_op jit(solution)/shard_map/exchange/pallas_call | solution.py:85
  174.6 0.0 copy-done.3
  174.6 0.0 copy-start.1
  174.6 3.4 %copy-done.1 = bf16[16,8,2,2,8,1024]{5,4,3,2,1,0:T(8,128)(2,1)S(1)} copy-done((bf16[16,8,2,2,8,1024]{5,4,3,2,1,0:T(8,128)(2,1)S(1)}, bf16[16,8,2,2,8,1024]{5,4,3,2,1,0:T(8,128)(2,1)}, u32[]{:S(2)}) %copy-start.1) | copy-done | bytes 8388632
  178.0 19.2 %attend.1 = (bf16[128,2,8,1024]{3,2,1,0:T(8,128)(2,1)}, bf16[64,64,128]{2,1,0:T(8,128)(2,1)S(1)}, f32[64,128]{1,0:T(8,128)S(1)}) custom-call(s32[64]{0:T(128)S(1)} %multiply_add_fusion.arrive_ref, s32[128]{0:T(128)S(1)} %reshape.180.table_ref, s32[64]{0:T(128)S(1)} %gather_fusion, bf16[128,2,2,8,1024]{4,3,2,1,0:T(8,128)(2,1)S(1)} %bitcast.29, ...), custom_call_target="tpu_custom_call" | custom-call | tf_op jit(solution)/shard_map/attend/pallas_call | solution.py:178
  197.2 0.0 copy-start.4
  197.2 1.7 copy.17
  198.9 0.0 copy-done.4
  198.9 30.1 %weights.1 = f32[8,128]{1,0:T(8,128)} custom-call(f32[64,128]{1,0:T(8,128)} %copy-done.4), custom_call_target="tpu_custom_call" | custom-call | tf_op jit(solution)/shard_map/weights/pallas_call | solution.py:261
  229.0 1.2 slice_bitcast_fusion
  (7 shorter events, 0.1 us)
Async XLA Ops:
  0.6 1.0 copy-start
  6.5 2.2 copy-start.2
  8.7 165.9 %copy-start.3 = (f32[8192]{0:T(1024)S(1)}, f32[8192]{0:T(1024)}, u32[]{:S(2)}) copy-start(f32[8192]{0:T(1024)} %param.13) | copy-start | bytes 98308
  174.6 3.4 %copy-start.1 = (bf16[16,8,2,2,8,1024]{5,4,3,2,1,0:T(8,128)(2,1)S(1)}, bf16[16,8,2,2,8,1024]{5,4,3,2,1,0:T(8,128)(2,1)}, u32[]{:S(2)}) copy-start(bf16[16,8,2,2,8,1024]{5,4,3,2,1,0:T(8,128)(2,1)} %exchange.1) | copy-start | bytes 25165828
  197.2 1.7 copy-start.4

commit v4 on v3

--- a/solution.py
+++ b/solution.py
@@ -16,9 +16,14 @@
 
 def exchange_kernel(
     devices, capacity, pages, row_ref, table_ref, pool_ref, held_ref,
-    stage, send_sem, recv_sem, own_sem,
+    cache, stage, send_sem, recv_sem, own_sem, pool_sem,
 ):
     me = lax.axis_index("particle")
+    half = devices // 2
+    own_half = me // half
+    place = lax.rem(me, half)
+    fetch = pltpu.make_async_copy(pool_ref, cache, pool_sem)
+    fetch.start()
     barrier = pltpu.get_barrier_semaphore()
 
     def greet(k, carry):
@@ -30,52 +35,61 @@
 
     lax.fori_loop(1, devices, greet, 0)
 
-    def fill(k):
-        base = lax.rem(me + k, devices) * capacity
+    def target(far, j):
+        return lax.rem(own_half + far, 2) * half + lax.rem(place + j, half)
+
+    def source(far, j):
+        return lax.rem(own_half + far, 2) * half + lax.rem(place + half - j, half)
+
+    def fill(far, j):
+        base = target(far, j) * capacity
         for c in range(capacity):
             row = row_ref[base + c]
             for i in range(pages):
-                stage[k, c, i] = pool_ref[table_ref[row * pages + i]]
-
-    def copy_to(k):
+                stage[far * half + j, c, i] = cache[table_ref[row * pages + i]]
+
+    def copy(far, j, block):
+        k = far * half + j
         return pltpu.make_async_remote_copy(
             src_ref=stage.at[k],
-            dst_ref=held_ref.at[me],
+            dst_ref=held_ref.at[block],
             send_sem=send_sem.at[k],
             recv_sem=recv_sem.at[k],
-            device_id={"particle": lax.rem(me + k, devices)},
+            device_id={"particle": target(far, j)},
             device_id_type=pl.DeviceIdType.MESH,
         )
 
-    def send(i, carry):
-        half = i // 2
-        odd = half % 2
-        step = (half + 1) // 2
-        far = devices // 2 + step - 2 * step * odd
-        near = (1 - odd) * (devices - 1 - half // 2) + odd * (1 + half // 2)
-        k = far + (i % 2) * (near - far)
-        fill(k)
-        copy_to(k).start()
-        return carry
-
-    def finish(k, carry):
-        source = lax.rem(me + devices - k, devices)
-        pltpu.make_async_remote_copy(
-            src_ref=stage.at[k],
-            dst_ref=held_ref.at[source],
-            send_sem=send_sem.at[k],
-            recv_sem=recv_sem.at[k],
-            device_id={"particle": lax.rem(me + k, devices)},
-            device_id_type=pl.DeviceIdType.MESH,
-        ).wait()
-        return carry
-
+    def send(far, j):
+        fill(far, j)
+        copy(far, j, me).start()
+
+    def both(q, carry):
+        send(1, 2 * q)
+        send(1, 2 * q + 1)
+        send(0, q + 1)
+        return carry
+
+    def rest(j, carry):
+        send(0, j)
+        return carry
+
+    def finish_far(j, carry):
+        copy(1, j, source(1, j)).wait()
+        return carry
+
+    def finish_near(j, carry):
+        copy(0, j, source(0, j)).wait()
+        return carry
+
+    fetch.wait()
     pl.semaphore_wait(barrier, devices - 1)
-    lax.fori_loop(0, devices - 1, send, 0)
-    fill(0)
+    lax.fori_loop(0, half // 2, both, 0)
+    lax.fori_loop(half // 2 + 1, half, rest, 0)
+    fill(0, 0)
     own = pltpu.make_async_copy(stage.at[0], held_ref.at[me], own_sem)
     own.start()
-    lax.fori_loop(1, devices, finish, 0)
+    lax.fori_loop(1, half, finish_near, 0)
+    lax.fori_loop(0, half, finish_far, 0)
     own.wait()
 
 
@@ -88,17 +102,19 @@
         in_specs=[
             pl.BlockSpec(memory_space=pltpu.SMEM),
             pl.BlockSpec(memory_space=pltpu.SMEM),
-            pl.BlockSpec(memory_space=pltpu.VMEM),
+            pl.BlockSpec(memory_space=pltpu.HBM),
         ],
         out_specs=pl.BlockSpec(memory_space=pltpu.HBM),
         scratch_shapes=[
+            pltpu.VMEM(pool.shape, pool.dtype),
             pltpu.VMEM((devices,) + block, pool.dtype),
             pltpu.SemaphoreType.DMA((devices,)),
             pltpu.SemaphoreType.DMA((devices,)),
             pltpu.SemaphoreType.DMA,
+            pltpu.SemaphoreType.DMA,
         ],
         compiler_params=pltpu.CompilerParams(
-            collective_id=1, has_side_effects=True, vmem_limit_bytes=48 << 20
+            collective_id=1, has_side_effects=True, vmem_limit_bytes=58 << 20
         ),
         name="exchange",
     )(source_row.reshape(-1), table, pool)
@@ -195,7 +211,7 @@
             pltpu.SemaphoreType.DMA((rows,)),
             pltpu.SemaphoreType.DMA,
         ],
-        compiler_params=pltpu.CompilerParams(vmem_limit_bytes=32 << 20),
+        compiler_params=pltpu.CompilerParams(vmem_limit_bytes=58 << 20),
         name="attend",
     )(arrive, table, length_now, held, query, fresh, weight)
 

time: 231 us -> 231 us (level)
    pallas_call x1, Pallas kernels: 166 us -> 188 us  [exchange(): pl.pallas_call(functools.partial(exchange_kernel, devices, capacity, page...]
    pallas_call x1, Pallas kernels: 30.1 us -> 11.5 us  [weights(): pl.pallas_call(functools.partial(weights_kernel, devices, prompts), out_s...]
    pallas_call x1, Pallas kernels: 19.2 us -> 16.2 us  [attend(): pl.pallas_call(functools.partial(attend_kernel, rows, pages), out_shape=(...]
    unnamed x14 -> x6, local copies, waits for them, and re-layouts: 10.6 us -> 7.94 us
where the time goes in v4:
time: 231 us
  Pallas kernels  216 us (94%)
  local copies, waits for them, and re-layouts  12.5 us (5%)
    pallas_call x1, Pallas kernels, exchange(): pl.pallas_call(functools.partial(exchange_kernel, devices, capacity, page...  188 us
    pallas_call x1, Pallas kernels, attend(): pl.pallas_call(functools.partial(attend_kernel, rows, pages), out_shape=(...  16.2 us
    pallas_call x1, Pallas kernels, weights(): pl.pallas_call(functools.partial(weights_kernel, devices, prompts), out_s...  11.5 us
    unnamed x6, local copies, waits for them, and re-layouts  7.94 us

profile of v4, /device:TPU:0, one launch (start us, length us, event | category | flops | bytes accessed | tf_op | source)
XLA Modules:
  0.0 230.6 jit_solution(16481168671407418689)
XLA Ops:
  0.6 0.0 copy-start
  0.6 0.8 reshape.179
  1.5 0.2 convert_reduce_fusion
  1.6 0.5 multiply_add_fusion.arrive_ref
  2.2 0.0 copy-done
  2.2 1.2 gather_fusion
  3.4 0.2 reduce_window_sum.11
  3.7 0.3 select_reduce_fusion
  4.0 0.6 reshape.181.row_ref
  4.6 0.8 copy.12
  5.4 0.7 reshape.180.table_ref
  6.1 1.8 copy.14
  7.9 2.5 %copy.13 = bf16[8,8,64,128]{3,2,1,0:T(8,128)(2,1)} copy(bf16[8,8,64,128]{3,1,2,0:T(8,128)(2,1)} %bitcast.32) | data formatting | bytes 2097152
  10.4 188.4 %exchange.1 = bf16[16,8,2,2,8,1024]{5,4,3,2,1,0:T(8,128)(2,1)} custom-call(s32[128]{0:T(128)} %reshape.181.row_ref, s32[128]{0:T(128)} %reshape.180.table_ref, bf16[128,2,8,1024]{3,2,1,0:T(8,128)(2,1)} %pool_ref.1), custom_call_target="tpu_custom_call" | custom-call | tf_op jit(solution)/shard_map/exchange/pallas_call | solution.py:99
  198.8 16.2 %attend.1 = (bf16[128,2,8,1024]{3,2,1,0:T(8,128)(2,1)}, bf16[64,64,128]{2,1,0:T(8,128)(2,1)}, f32[64,128]{1,0:T(8,128)}) custom-call(s32[64]{0:T(128)} %multiply_add_fusion.arrive_ref, s32[128]{0:T(128)} %reshape.180.table_ref, s32[64]{0:T(128)} %gather_fusion, bf16[128,2,2,8,1024]{4,3,2,1,0:T(8,128)(2,1)} %bitcast.29, bf16[64,64,128]{2,1,0:T(8,128)(2,1)} %bitcast.30, ...), custom_call_target="tpu_custom_call" | custom-call | tf_op jit(solution)/shard_map/attend/pallas_call | solution.py:194
  215.1 2.9 %copy.17 = bf16[8,8,64,128]{3,1,2,0:T(8,128)(2,1)} copy(bf16[8,8,64,128]{3,2,1,0:T(8,128)(2,1)} %bitcast.34) | data formatting | bytes 2097152
  218.0 11.5 %weights.1 = f32[8,128]{1,0:T(8,128)} custom-call(f32[64,128]{1,0:T(8,128)} %get-tuple-element.8.part_ref), custom_call_target="tpu_custom_call" | custom-call | tf_op jit(solution)/shard_map/weights/pallas_call | solution.py:277
  229.4 1.2 slice_bitcast_fusion
  (6 shorter events, 0.1 us)
Async XLA Ops:
  0.6 1.5 copy-start

commit v5 on v3

--- a/solution.py
+++ b/solution.py
@@ -11,7 +11,7 @@
 KV_HEADS = 8
 HEAD_DIM = 128
 GROUP = 64
-BATCH = 16
+BATCH = 8
 
 
 def exchange_kernel(
@@ -195,7 +195,7 @@
             pltpu.SemaphoreType.DMA((rows,)),
             pltpu.SemaphoreType.DMA,
         ],
-        compiler_params=pltpu.CompilerParams(vmem_limit_bytes=32 << 20),
+        compiler_params=pltpu.CompilerParams(vmem_limit_bytes=52 << 20),
         name="attend",
     )(arrive, table, length_now, held, query, fresh, weight)
 

time: 231 us -> 225 us (0.974)
  Pallas kernels: 215 us -> 212 us
    pallas_call x1, Pallas kernels: 19.2 us -> 15.9 us  [attend(): pl.pallas_call(functools.partial(attend_kernel, rows, pages), out_shape=(...]
    unnamed x14 -> x12, local copies, waits for them, and re-layouts: 10.6 us -> 8.16 us
where the time goes in v5:
time: 225 us; the launch traced here: 224 us
  Pallas kernels  212 us (94%)
  local copies, waits for them, and re-layouts  11.1 us (5%)
    pallas_call x1, Pallas kernels, exchange(): pl.pallas_call(functools.partial(exchange_kernel, devices, capacity, page...  166 us
    pallas_call x1, Pallas kernels, weights(): pl.pallas_call(functools.partial(weights_kernel, devices, prompts), out_s...  30.1 us
    pallas_call x1, Pallas kernels, attend(): pl.pallas_call(functools.partial(attend_kernel, rows, pages), out_shape=(...  15.9 us
    unnamed x12, local copies, waits for them, and re-layouts  8.16 us

profile of v5, /device:TPU:0, one launch (start us, length us, event | category | flops | bytes accessed | tf_op | source)
XLA Modules:
  0.0 224.5 jit_solution(11476261231757310838)
XLA Ops:
  0.6 0.0 copy-start
  0.6 0.8 reshape.179
  1.5 0.2 convert_reduce_fusion
  1.7 0.0 copy-done
  1.7 0.7 gather_fusion
  2.4 0.2 reduce_window_sum.11
  2.7 0.3 select_reduce_fusion
  3.0 0.1 reshape.181.row_ref
  3.1 0.8 copy.12
  3.9 0.1 reshape.180.table_ref
  4.0 1.0 copy.14
  5.0 2.5 %copy.13 = bf16[8,8,64,128]{3,2,1,0:T(8,128)(2,1)} copy(bf16[8,8,64,128]{3,1,2,0:T(8,128)(2,1)} %bitcast.34) | data formatting | bytes 2097152
  7.5 0.0 copy-start.1
  7.5 2.2 copy-done.1
  9.7 0.0 copy-start.2
  9.7 165.9 %exchange.1 = bf16[16,8,2,2,8,1024]{5,4,3,2,1,0:T(8,128)(2,1)} custom-call(s32[128]{0:T(128)S(1)} %reshape.181.row_ref, s32[128]{0:T(128)S(1)} %reshape.180.table_ref, bf16[128,2,8,1024]{3,2,1,0:T(8,128)(2,1)S(1)} %copy-done.1), custom_call_target="tpu_custom_call" | custom-call | tf_op jit(solution)/shard_map/exchange/pallas_call | solution.py:85
  175.6 0.0 copy-done.2
  175.6 15.9 %attend.1 = (bf16[128,2,8,1024]{3,2,1,0:T(8,128)(2,1)}, bf16[64,64,128]{2,1,0:T(8,128)(2,1)S(1)}, f32[64,128]{1,0:T(8,128)S(1)}) custom-call(s32[64]{0:T(128)S(1)} %multiply_add_fusion.arrive_ref, s32[128]{0:T(128)S(1)} %reshape.180.table_ref, s32[64]{0:T(128)S(1)} %gather_fusion, bf16[128,2,2,8,1024]{4,3,2,1,0:T(8,128)(2,1)} %bitcast.32, ...), custom_call_target="tpu_custom_call" | custom-call | tf_op jit(solution)/shard_map/attend/pallas_call | solution.py:178
  191.5 0.0 copy-start.3
  191.5 1.7 copy.17
  193.2 0.0 copy-done.3
  193.2 30.1 %weights.1 = f32[8,128]{1,0:T(8,128)} custom-call(f32[64,128]{1,0:T(8,128)} %copy-done.3), custom_call_target="tpu_custom_call" | custom-call | tf_op jit(solution)/shard_map/weights/pallas_call | solution.py:261
  223.3 1.2 slice_bitcast_fusion
  (7 shorter events, 0.1 us)
Async XLA Ops:
  0.6 1.0 copy-start
  7.5 2.2 copy-start.1
  9.7 165.9 %copy-start.2 = (f32[8192]{0:T(1024)S(1)}, f32[8192]{0:T(1024)}, u32[]{:S(2)}) copy-start(f32[8192]{0:T(1024)} %param.13) | copy-start | bytes 98308
  191.5 1.7 copy-start.3

commit v6 on v5

--- a/solution.py
+++ b/solution.py
@@ -296,6 +296,7 @@
     )
     source_row = jnp.sum(jnp.where(picked, anc_all[:, None, :] % per_device, 0), axis=2)
     incoming = exchange(pool, table, source_row, page_count)
+    incoming, new_q, new_kv = lax.optimization_barrier((incoming, new_q, new_kv))
     incoming = incoming.reshape((devices * capacity,) + incoming.shape[2:])
     earlier = (my_sources[None, :] == my_sources[:, None]) & (
         row_order[None, :] < row_order[:, None]

time: 225 us -> 223 us (level)
    unnamed x12 -> x16, local copies, waits for them, and re-layouts: 8.16 us -> 5.99 us
where the time goes in v6:
time: 223 us; the launch traced here: 222 us
  Pallas kernels  212 us (95%)
  local copies, waits for them, and re-layouts  8.89 us (4%)
    pallas_call x1, Pallas kernels, exchange(): pl.pallas_call(functools.partial(exchange_kernel, devices, capacity, page...  166 us
    pallas_call x1, Pallas kernels, weights(): pl.pallas_call(functools.partial(weights_kernel, devices, prompts), out_s...  30.1 us
    pallas_call x1, Pallas kernels, attend(): pl.pallas_call(functools.partial(attend_kernel, rows, pages), out_shape=(...  15.9 us
    unnamed x16, local copies, waits for them, and re-layouts  5.99 us

profile of v6, /device:TPU:0, one launch (start us, length us, event | category | flops | bytes accessed | tf_op | source)
XLA Modules:
  0.0 222.3 jit_solution(6464354877687715694)
XLA Ops:
  0.6 0.0 copy-start
  0.6 0.8 reshape.179
  1.5 0.2 convert_reduce_fusion
  1.7 0.0 copy-done
  1.7 0.7 gather_fusion
  2.4 0.2 reduce_window_sum.11
  2.7 0.3 select_reduce_fusion
  3.0 0.1 reshape.181.row_ref
  3.1 0.8 copy.12
  3.9 0.1 reshape.180.table_ref
  4.0 0.0 copy-start.1
  4.0 2.2 copy-done.1
  6.2 0.0 copy-start.5
  6.2 0.0 copy-start.4
  6.2 0.0 copy-start.2
  6.2 165.9 %exchange.1 = bf16[16,8,2,2,8,1024]{5,4,3,2,1,0:T(8,128)(2,1)} custom-call(s32[128]{0:T(128)S(1)} %reshape.181.row_ref, s32[128]{0:T(128)S(1)} %reshape.180.table_ref, bf16[128,2,8,1024]{3,2,1,0:T(8,128)(2,1)S(1)} %copy-done.1), custom_call_target="tpu_custom_call" | custom-call | tf_op jit(solution)/shard_map/exchange/pallas_call | solution.py:85
  172.1 0.0 copy-done.5
  172.1 0.1 copy.14
  172.2 0.0 copy-done.4
  172.2 1.3 copy.13
  173.4 0.0 copy-done.2
  173.4 15.9 %attend.1 = (bf16[128,2,8,1024]{3,2,1,0:T(8,128)(2,1)}, bf16[64,64,128]{2,1,0:T(8,128)(2,1)S(1)}, f32[64,128]{1,0:T(8,128)S(1)}) custom-call(s32[64]{0:T(128)S(1)} %multiply_add_fusion.arrive_ref, s32[128]{0:T(128)S(1)} %reshape.180.table_ref, s32[64]{0:T(128)S(1)} %gather_fusion, bf16[128,2,2,8,1024]{4,3,2,1,0:T(8,128)(2,1)} %bitcast.32, ...), custom_call_target="tpu_custom_call" | custom-call | tf_op jit(solution)/shard_map/attend/pallas_call | solution.py:178
  189.3 0.0 copy-start.3
  189.4 1.7 copy.17
  191.0 0.0 copy-done.3
  191.0 30.1 %weights.1 = f32[8,128]{1,0:T(8,128)} custom-call(f32[64,128]{1,0:T(8,128)} %copy-done.3), custom_call_target="tpu_custom_call" | custom-call | tf_op jit(solution)/shard_map/weights/pallas_call | solution.py:261
  221.1 1.2 slice_bitcast_fusion
  (7 shorter events, 0.1 us)
Async XLA Ops:
  0.6 1.0 copy-start
  4.0 2.2 copy-start.1
  6.2 165.9 %copy-start.5 = (bf16[64,2,1024]{2,1,0:T(2,128)(2,1)S(1)}, bf16[64,2,1024]{2,1,0:T(2,128)(2,1)}, u32[]{:S(2)}) copy-start(bf16[64,2,1024]{2,1,0:T(2,128)(2,1)} %param.12) | copy-start | bytes 786436
  6.2 165.9 %copy-start.4 = (bf16[64,8192]{1,0:T(8,128)(2,1)S(1)}, bf16[64,8192]{1,0:T(8,128)(2,1)}, u32[]{:S(2)}) copy-start(bf16[64,8192]{1,0:T(8,128)(2,1)} %param.11) | copy-start | bytes 3145732
  6.2 167.2 %copy-start.2 = (f32[8192]{0:T(1024)S(1)}, f32[8192]{0:T(1024)}, u32[]{:S(2)}) copy-start(f32[8192]{0:T(1024)} %param.13) | copy-start | bytes 98308
  189.3 1.7 copy-start.3
